TPU v7x, 256 devices: a whole 4x4x8 slice. The times are simulated.
256 devices in a mesh: pop: 32 (over z, x_hi, core), hid: 8 (over y, x_lo).
Axes of the slice: x: 4 (x_hi: 2, x_lo: 2; x = x_hi * 2 + x_lo), y: 4, z: 8, core: 2. Of those that a mesh axis runs over, the one named last changes fastest.
Arguments:
- tokens: bfloat16 [1024, 4096], P('pop', 'hid'), may hold values from -6 to 6
- fitness_ranks: int32 [64], replicated, may hold values from 0 to 63, each once
- gate_weight: bfloat16 [4096, 16384], P('hid', 'pop'), may hold values from -0.09375 to 0.09375
- up_weight: bfloat16 [4096, 16384], P('hid', 'pop'), may hold values from -0.09375 to 0.09375
- down_weight: bfloat16 [16384, 4096], P('pop', 'hid'), may hold values from -0.046875 to 0.046875
- gate_input_factor: bfloat16 [64, 4, 4096], P(None, None, 'hid'), may hold values from -6 to 6
- up_input_factor: bfloat16 [64, 4, 4096], P(None, None, 'hid'), may hold values from -6 to 6
- down_right: bfloat16 [64, 4, 4096], P(None, None, 'hid'), may hold values from -6 to 6
- gate_output_factor: bfloat16 [64, 4, 16384], P('pop'), may hold values from -6 to 6
- up_output_factor: bfloat16 [64, 4, 16384], P('pop'), may hold values from -6 to 6
- down_left: bfloat16 [64, 4, 16384], P('pop'), may hold values from -6 to 6
Outputs:
- mixed: bfloat16 [1024, 4096], P('pop', 'hid')
- gate_step: float32 [4096, 16384], P('hid', 'pop')
- up_step: float32 [4096, 16384], P('hid', 'pop')
- down_step: float32 [16384, 4096], P('pop', 'hid')
Inputs may be any that keep to these rules, and one draw needn't show every extreme that they name: `fitness_ranks`: every rank appears exactly once.
All inputs are finite; a program needn't handle non-finite values.
Results may differ from a plain program's by a relative error of at most 0.025.
Values may be sent and summed in bfloat16 or wider, within the bound.
A program may use at most 64 MiB of HBM per device.

v0:
```python
import math

import jax
import jax.numpy as jnp
from jax import lax
from jax.sharding import PartitionSpec as P

MODEL_WIDTH = 4096
HIDDEN_UNITS = 16384
RANK = 4
SAMPLE_LENGTH = 16


def copy_for_each(x, axis):
    copies = jnp.broadcast_to(x, (lax.axis_size(axis), *x.shape))
    return lax.all_to_all(copies, axis, split_axis=0, concat_axis=0, tiled=True)


def of_everyone(x, axis):
    return copy_for_each(x, axis).sum(axis=0)


def in_one(arrays, axis):
    flat, at, gathered = (jnp.concatenate([a.reshape(-1) for a in arrays]), 0, [])
    total = of_everyone(flat, axis)
    for a in arrays:
        gathered.append(total[at : at + a.size].reshape(a.shape))
        at += a.size
    return tuple(gathered)


def in_one_piece(arrays, axis, dim, along):
    both = jnp.concatenate(arrays, axis=along)
    whole, at, gathered = (lax.all_gather(both, axis, axis=dim, tiled=True), 0, [])
    for a in arrays:
        gathered.append(lax.slice_in_dim(whole, at, at + a.shape[along], axis=along))
        at += a.shape[along]
    return tuple(gathered)


def sent_together(arrays, axis, split_dim, concat_dim, along):
    both = jnp.concatenate(arrays, axis=along)
    whole, at, gathered = (
        lax.all_to_all(both, axis, split_axis=split_dim, concat_axis=concat_dim, tiled=True),
        0,
        [],
    )
    for a in arrays:
        gathered.append(lax.slice_in_dim(whole, at, at + a.shape[along], axis=along))
        at += a.shape[along]
    return tuple(gathered)


def in_order(blocks, dim):
    blocks = jnp.moveaxis(blocks, 0, dim)
    lengths = blocks.shape
    return blocks.reshape(*lengths[:dim], lengths[dim] * lengths[dim + 1], *lengths[dim + 2 :])


def gather_directly(x, axis, dim):
    return in_order(copy_for_each(x, axis), dim)


def split_up(x, dim, size):
    before, after = (x.shape[:dim], x.shape[dim + 1 :])
    return jnp.moveaxis(x.reshape(*before, size, -1, *after), dim, 0)


def sum_at_owner(x, axis, dim):
    size = lax.axis_size(axis)
    blocks = lax.all_to_all(split_up(x, dim, size), axis, 0, 0, tiled=True)
    return jnp.sum(blocks.astype(jnp.float32), axis=0)


def local(
    tokens,
    fitness_ranks,
    gate_weight,
    up_weight,
    down_weight,
    gate_input_factor,
    up_input_factor,
    down_right,
    gate_output_factor,
    up_output_factor,
    down_left,
):
    scalar_real = jnp.float32
    pop_count = lax.axis_size("pop")
    hid_count = lax.axis_size("hid")
    pop_index = lax.axis_index("pop")
    hid_index = lax.axis_index("hid")
    tok_local = tokens.shape[0]
    mem_local = tok_local // SAMPLE_LENGTH
    members = mem_local * pop_count
    total_rows = tok_local * pop_count
    row_block_count = total_rows // hid_count
    block_members = row_block_count // SAMPLE_LENGTH
    width_part = tokens.shape[1]
    hidden_portion = gate_weight.shape[1]
    scale_in = 0.5 / math.sqrt(MODEL_WIDTH * RANK)
    scale_out = 0.5 / math.sqrt(HIDDEN_UNITS * RANK)
    fitness = fitness_ranks.astype(scalar_real) / (members - 1) - 0.5
    member_token_rows = tokens.reshape(mem_local, SAMPLE_LENGTH, width_part)
    member_gate_input = lax.dynamic_slice_in_dim(
        gate_input_factor, pop_index * mem_local, mem_local, 0
    )
    member_up_input = lax.dynamic_slice_in_dim(up_input_factor, pop_index * mem_local, mem_local, 0)
    gate_projection = jnp.einsum(
        "otl,ozl->otz", member_token_rows, member_gate_input, preferred_element_type=scalar_real
    )
    up_projection = jnp.einsum(
        "otl,ozl->otz", member_token_rows, member_up_input, preferred_element_type=scalar_real
    )
    gate_projection, up_projection = in_one((gate_projection, up_projection), "hid")
    gate_projection, up_projection = in_one_piece((gate_projection, up_projection), "pop", 0, 1)
    gate_cols, up_cols, down_cols = sent_together(
        (gate_output_factor, up_output_factor, down_left), "pop", 2, 0, 1
    )
    gathered = gather_directly(tokens, "pop", 0)
    paired = jnp.concatenate([gate_weight, up_weight], axis=1)
    picked = gathered
    sums = lax.psum_scatter(
        jnp.dot(picked, paired, preferred_element_type=scalar_real).astype(jnp.bfloat16),
        "hid",
        scatter_dimension=0,
        tiled=True,
    ).astype(jnp.float32)
    gate_sum = sums[:, :hidden_portion]
    up_sum = sums[:, hidden_portion:]
    first_member = hid_index * block_members
    gate_tile_block = lax.dynamic_slice_in_dim(gate_projection, first_member, block_members, 0)
    up_tile_block = lax.dynamic_slice_in_dim(up_projection, first_member, block_members, 0)
    gate_vectors = lax.dynamic_slice_in_dim(gate_cols, first_member, block_members, 0).astype(
        scalar_real
    )
    up_vectors = lax.dynamic_slice_in_dim(up_cols, first_member, block_members, 0).astype(
        scalar_real
    )
    gate_lowrank_term = jnp.einsum("iln,ina->ila", gate_tile_block, gate_vectors).reshape(
        row_block_count, hidden_portion
    )
    up_lowrank_term = jnp.einsum("iln,ina->ila", up_tile_block, up_vectors).reshape(
        row_block_count, hidden_portion
    )
    gate = gate_sum + scale_in * gate_lowrank_term
    up = up_sum + scale_in * up_lowrank_term
    hidden = (jax.nn.silu(gate) * up).astype(jnp.bfloat16)
    every_hidden = gather_directly(hidden, "hid", 0)
    picked = every_hidden
    member_count = tok_local * lax.axis_size("pop") // SAMPLE_LENGTH
    output_factor_portion = down_right.astype(scalar_real)
    contracting_matrix = jnp.einsum(
        "reu,ryu->rey",
        picked.reshape(member_count, SAMPLE_LENGTH, hidden_portion),
        down_cols,
        preferred_element_type=scalar_real,
    )
    lowrank_product = jnp.einsum("okw,owt->okt", contracting_matrix, output_factor_portion).reshape(
        tok_local * lax.axis_size("pop"), width_part
    )
    mixed = sum_at_owner(
        (
            jnp.dot(picked, down_weight, preferred_element_type=scalar_real)
            + scale_out * lowrank_product
        ).astype(jnp.bfloat16),
        "pop",
        0,
    ).astype(jnp.bfloat16)
    factor = 1.0 / math.sqrt(members * RANK)
    weights3 = fitness[:, None, None]
    scaled_gate = (
        (gate_input_factor.astype(scalar_real) * weights3)
        .astype(jnp.bfloat16)
        .reshape(members * RANK, width_part)
    )
    scaled_up = (
        (up_input_factor.astype(scalar_real) * weights3)
        .astype(jnp.bfloat16)
        .reshape(members * RANK, width_part)
    )
    scaled_down = (
        (down_right.astype(scalar_real) * weights3)
        .astype(jnp.bfloat16)
        .reshape(members * RANK, width_part)
    )
    dims = (((0,), (0,)), ((), ()))
    gate_step = factor * lax.dot_general(
        scaled_gate,
        gate_cols.reshape(members * RANK, hidden_portion),
        dims,
        preferred_element_type=scalar_real,
    )
    up_step = factor * lax.dot_general(
        scaled_up,
        up_cols.reshape(members * RANK, hidden_portion),
        dims,
        preferred_element_type=scalar_real,
    )
    down_step = factor * lax.dot_general(
        down_cols.reshape(members * RANK, hidden_portion),
        scaled_down,
        dims,
        preferred_element_type=scalar_real,
    )
    return (mixed, gate_step, up_step, down_step)


def solution(mesh):
    in_specs = (
        P("pop", "hid"),
        P(),
        P("hid", "pop"),
        P("hid", "pop"),
        P("pop", "hid"),
        P(None, None, "hid"),
        P(None, None, "hid"),
        P(None, None, "hid"),
        P("pop", None, None),
        P("pop", None, None),
        P("pop", None, None),
    )
    out_specs = (P("pop", "hid"), P("hid", "pop"), P("hid", "pop"), P("pop", "hid"))
    return jax.shard_map(local, mesh=mesh, in_specs=in_specs, out_specs=out_specs, check_vma=False)
```

profile of v0, /device:TPU:32, one launch (start us, length us, event | category | flops | bytes accessed | tf_op | source)
XLA Modules:
  0.0 263.9 jit_solution(15197976784383680324)
XLA Ops:
  7.2 1.9 broadcast_in_dim.10
  9.1 11.2 %all-to-all-start = ((bf16[32,32,512]{2,1,0:T(8,128)(2,1)}), bf16[32,32,512]{2,1,0:T(8,128)(2,1)S(1)}, u32[]{:S(2)}, u32[]{:S(2)}) async-start(bf16[32,32,512]{2,1,0:T(8,128)(2,1)} %broadcast_in_dim.10), calls=%async_computation | async-start | bytes 2097152 | tf_op jit(solution)/shard_map/all_to_all | solution.py:16
  20.4 28.0 %all-to-all-done = bf16[32,32,512]{2,1,0:T(8,128)(2,1)S(1)} async-done(((bf16[32,32,512]{2,1,0:T(8,128)(2,1)}), bf16[32,32,512]{2,1,0:T(8,128)(2,1)S(1)}, u32[]{:S(2)}, u32[]{:S(2)}) %all-to-all-start) | async-done | bytes 1048608 | tf_op jit(solution)/shard_map/all_to_all | solution.py:16
  48.4 1.0 copy-done.1
  49.3 2.7 %convert_bitcast_fusion = bf16[1024,1024]{0,1:T(8,128)(2,1)S(1)} fusion(bf16[1024,512]{1,0:T(8,128)(2,1)} %bitcast.53, bf16[512,512]{1,0:T(8,128)(2,1)S(1)} %copy-done.10, bf16[512,512]{1,0:T(8,128)(2,1)} %param.13), kind=kOutput, calls=%fused_computation.2 | convolution fusion | flops 1076887552 | bytes 4194304 | tf_op jit(solution)/shard_map/dot_general | solution.py:124
  52.0 2.7 %copy.97 = bf16[1024,1024]{1,0:T(8,128)(2,1)} copy(bf16[1024,1024]{0,1:T(8,128)(2,1)S(1)} %convert_bitcast_fusion) | data formatting | bytes 4194304
  56.5 0.8 convolution_bitcast_fusion.3
  58.1 4.5 %all-to-all-start.1 = ((f32[8,1,256]{2,1,0:T(1,128)}), f32[8,1,256]{2,1,0:T(1,128)S(1)}, u32[]{:S(2)}, u32[]{:S(2)}) async-start(f32[8,1,256]{2,1,0:T(1,128)} %broadcast_in_dim.11), calls=%async_computation.1 | async-start | bytes 16384 | tf_op jit(solution)/shard_map/all_to_all | solution.py:16
  63.1 13.1 %copy.89 = bf16[2,12,16384]{1,0,2:T(2,128)(2,1)} copy(bf16[2,12,16384]{2,1,0:T(8,128)(2,1)S(1)} %pad_maximum_fusion) | data formatting | bytes 1572864 | tf_op jit(solution)/shard_map/concatenate | solution.py:42
  76.2 17.3 %reshape.81 = bf16[32,2,6144]{2,1,0:T(2,128)(2,1)} reshape(bf16[16384,2,12]{2,1,0:T(2,128)(2,1)} %bitcast.47) | data formatting | bytes 1572864
  93.5 6.5 %all-to-all-start.2 = ((bf16[32,2,6144]{2,1,0:T(2,128)(2,1)}), bf16[32,2,6144]{2,1,0:T(2,128)(2,1)S(1)}, u32[]{:S(2)}, u32[]{:S(2)}) async-start(bf16[32,2,6144]{2,1,0:T(2,128)(2,1)} %reshape.81), calls=%async_computation.2 | async-start | bytes 1572864 | tf_op jit(solution)/shard_map/all_to_all | solution.py:44
  100.5 48.4 %all_gather.3 = bf16[64,32,4]{1,2,0:T(4,128)(2,1)S(1)} all-gather(bf16[2,32,4]{1,2,0:T(4,128)(2,1)S(1)} %pad_maximum_fusion.1), channel_id=1, replica_groups=mesh['pop'=32,'hid'=8] {'pop'}, dimensions={0}, use_global_device_ids=true | all-gather | bytes 16896 | tf_op jit(solution)/shard_map/all_gather | solution.py:34
  149.1 20.4 %reshape.82 = bf16[16384,2,12]{2,1,0:T(2,128)(2,1)} reshape(bf16[32,2,6144]{2,1,0:T(2,128)(2,1)S(1)} %all-to-all-done.2) | data formatting | bytes 1572864
  169.5 17.9 %copy.90 = bf16[2,12,32,512]{3,1,0,2:T(8,128)(2,1)S(1)} copy(bf16[2,12,32,512]{1,0,3,2:T(2,128)(2,1)} %bitcast.48) | data formatting | bytes 1572864 | tf_op jit(solution)/shard_map/all_to_all | solution.py:44
  187.4 0.9 fusion.30
  188.9 1.0 convert_element_type.43
  190.1 21.1 %all_to_all.39 = bf16[8,128,512]{2,1,0:T(8,128)(2,1)S(1)} all-to-all(bf16[8,128,512]{2,1,0:T(8,128)(2,1)S(1)} %broadcast_in_dim.12), channel_id=1, replica_groups=mesh['pop'=32,'hid'=8] {'hid'}, dimensions={0} | all-to-all | bytes 2097152 | tf_op jit(solution)/shard_map/all_to_all | solution.py:16
  211.2 2.1 convolution_multiply_fusion
  213.3 3.3 %fusion = bf16[1024,512]{1,0:T(8,128)(2,1)} fusion(f32[64,16,512]{2,1,0:T(8,128)} %convolution_multiply_fusion, bf16[1024,512]{1,0:T(8,128)(2,1)S(1)} %bitcast.50, bf16[512,512]{1,0:T(8,128)(2,1)S(1)} %copy-done), kind=kOutput, calls=%fused_computation.1 | convolution fusion | flops 537919488 | bytes 4718592 | tf_op jit(solution)/shard_map/dot_general | solution.py:164
  216.5 11.7 %all-to-all-start.4 = ((bf16[32,32,512]{2,1,0:T(8,128)(2,1)}), bf16[32,32,512]{2,1,0:T(8,128)(2,1)S(1)}, u32[]{:S(2)}, u32[]{:S(2)}) async-start(bf16[32,32,512]{2,1,0:T(8,128)(2,1)} %bitcast.14), calls=%async_computation.4 | async-start | bytes 2097152 | tf_op jit(solution)/shard_map/all_to_all | solution.py:71
  228.7 1.3 fusion.2
  230.0 1.3 fusion.3
  231.3 1.3 fusion.1
  232.6 23.7 %all-to-all-done.4 = bf16[32,32,512]{2,1,0:T(8,128)(2,1)S(1)} async-done(((bf16[32,32,512]{2,1,0:T(8,128)(2,1)}), bf16[32,32,512]{2,1,0:T(8,128)(2,1)S(1)}, u32[]{:S(2)}, u32[]{:S(2)}) %all-to-all-start.4) | async-done | bytes 1048608 | tf_op jit(solution)/shard_map/all_to_all | solution.py:71
  (51 shorter events, 5.6 us)
Async XLA Ops:
  7.2 206.1 %copy-start = (bf16[512,512]{1,0:T(8,128)(2,1)S(1)}, bf16[512,512]{1,0:T(8,128)(2,1)}, u32[]{:S(2)}) copy-start(bf16[512,512]{1,0:T(8,128)(2,1)} %param.15) | copy-start | bytes 1572868
  7.2 42.2 %copy-start.10 = (bf16[512,512]{1,0:T(8,128)(2,1)S(1)}, bf16[512,512]{1,0:T(8,128)(2,1)}, u32[]{:S(2)}) copy-start(bf16[512,512]{1,0:T(8,128)(2,1)} %param.14) | copy-start | bytes 1572868
  9.1 39.2 %all-to-all-start = ((bf16[32,32,512]{2,1,0:T(8,128)(2,1)}), bf16[32,32,512]{2,1,0:T(8,128)(2,1)S(1)}, u32[]{:S(2)}, u32[]{:S(2)}) async-start(bf16[32,32,512]{2,1,0:T(8,128)(2,1)} %broadcast_in_dim.10), calls=%async_computation | async-start | bytes 2097152 | tf_op jit(solution)/shard_map/all_to_all | solution.py:16
  20.3 168.6 %reduce-scatter.4.cloned.1.call-start = ((), (), s32[]{:S(2)}) async-start(), calls=%async_computation.6 | async-start | bytes 2359296 | tf_op jit(solution)/shard_map/reduce_scatter | solution.py:123
  48.4 1.0 copy-start.1
  54.7 0.8 copy-start.3
  54.7 7.9 %copy-start.6 = (bf16[2,4,16384]{2,1,0:T(4,128)(2,1)S(1)}, bf16[2,4,16384]{2,1,0:T(4,128)(2,1)}, u32[]{:S(2)}) copy-start(bf16[2,4,16384]{2,1,0:T(4,128)(2,1)} %param.21) | copy-start | bytes 786436
  54.7 7.9 %copy-start.7 = (bf16[2,4,16384]{2,1,0:T(4,128)(2,1)S(1)}, bf16[2,4,16384]{2,1,0:T(4,128)(2,1)}, u32[]{:S(2)}) copy-start(bf16[2,4,16384]{2,1,0:T(4,128)(2,1)} %param.20) | copy-start | bytes 786436
  54.7 7.9 %copy-start.8 = (bf16[2,4,16384]{2,1,0:T(4,128)(2,1)S(1)}, bf16[2,4,16384]{2,1,0:T(4,128)(2,1)}, u32[]{:S(2)}) copy-start(bf16[2,4,16384]{2,1,0:T(4,128)(2,1)} %param.19) | copy-start | bytes 786436
  58.1 35.3 %all-to-all-start.1 = ((f32[8,1,256]{2,1,0:T(1,128)}), f32[8,1,256]{2,1,0:T(1,128)S(1)}, u32[]{:S(2)}, u32[]{:S(2)}) async-start(f32[8,1,256]{2,1,0:T(1,128)} %broadcast_in_dim.11), calls=%async_computation.1 | async-start | bytes 16384 | tf_op jit(solution)/shard_map/all_to_all | solution.py:16
  93.5 55.6 %all-to-all-start.2 = ((bf16[32,2,6144]{2,1,0:T(2,128)(2,1)}), bf16[32,2,6144]{2,1,0:T(2,128)(2,1)S(1)}, u32[]{:S(2)}, u32[]{:S(2)}) async-start(bf16[32,2,6144]{2,1,0:T(2,128)(2,1)} %reshape.81), calls=%async_computation.2 | async-start | bytes 1572864 | tf_op jit(solution)/shard_map/all_to_all | solution.py:44
  189.9 21.3 %copy-start.2 = (bf16[64,4,512]{2,1,0:T(4,128)(2,1)S(1)}, bf16[64,4,512]{2,1,0:T(4,128)(2,1)}, u32[]{:S(2)}) copy-start(bf16[64,4,512]{2,1,0:T(4,128)(2,1)} %param.18) | copy-start | bytes 786436
  216.5 11.7 %copy-start.11 = (s32[64]{0:T(128)S(1)}, s32[64]{0:T(128)}, u32[]{:S(2)}) copy-start(s32[64]{0:T(128)} %param.12) | copy-start | bytes 772
  216.5 11.8 %copy-start.4 = (bf16[64,4,512]{2,1,0:T(4,128)(2,1)S(1)}, bf16[64,4,512]{2,1,0:T(4,128)(2,1)}, u32[]{:S(2)}) copy-start(bf16[64,4,512]{2,1,0:T(4,128)(2,1)} %param.17) | copy-start | bytes 786436
  216.5 11.8 %copy-start.5 = (bf16[64,4,512]{2,1,0:T(4,128)(2,1)S(1)}, bf16[64,4,512]{2,1,0:T(4,128)(2,1)}, u32[]{:S(2)}) copy-start(bf16[64,4,512]{2,1,0:T(4,128)(2,1)} %param.16) | copy-start | bytes 786436
  216.5 39.8 %all-to-all-start.4 = ((bf16[32,32,512]{2,1,0:T(8,128)(2,1)}), bf16[32,32,512]{2,1,0:T(8,128)(2,1)S(1)}, u32[]{:S(2)}, u32[]{:S(2)}) async-start(bf16[32,32,512]{2,1,0:T(8,128)(2,1)} %bitcast.14), calls=%async_computation.4 | async-start | bytes 2097152 | tf_op jit(solution)/shard_map/all_to_all | solution.py:71
  228.3 3.0 %copy-start.9 = (bf16[64,4,512]{2,1,0:T(4,128)(2,1)S(1)}, bf16[64,4,512]{2,1,0:T(4,128)(2,1)}, u32[]{:S(2)}) copy-start(bf16[64,4,512]{2,1,0:T(4,128)(2,1)} %get-tuple-element.4) | copy-start | bytes 786436
Sparse Core Ops, SparseCore 0:
  54.9 54.8 reduce-scatter.3
where the time goes:
time: 266 us; the launch traced here: 264 us
  local copies, waits for them, and re-layouts  77.6 us (29%)
  blocking collectives  69.5 us (26%)
  waiting for transfers between devices  51.7 us (19%)
  starting transfers between devices  33.9 us (13%)
  between operations  14.3 us (5%)
  matrix products  14 us (5%)
  other arithmetic  2.82 us (1%)
    all_gather x1, blocking collectives, in_one_piece(): lax.all_gather(both, axis, axis=dim, tiled=True)  48.4 us
    unnamed x27, local copies, waits for them, and re-layouts  42.1 us
    all_to_all x2, waiting for transfers between devices, copy_for_each(): return lax.all_to_all(copies, axis, split_axis=0, concat_axis=0, tiled=True)  28 us
    all_to_all x1, waiting for transfers between devices, sum_at_owner(): blocks = lax.all_to_all(split_up(x, dim, size), axis, 0, 0, tiled=True)  23.7 us
    all_to_all x1, blocking collectives, copy_for_each(): return lax.all_to_all(copies, axis, split_axis=0, concat_axis=0, tiled=True)  21.1 us
    all_to_all x1, local copies, waits for them, and re-layouts, sent_together(): lax.all_to_all(both, axis, split_axis=split_dim, concat_axis=concat_dim,...  17.9 us
    all_to_all x2, starting transfers between devices, copy_for_each(): return lax.all_to_all(copies, axis, split_axis=0, concat_axis=0, tiled=True)  15.7 us
    concatenate x1, local copies, waits for them, and re-layouts, sent_together(): both = jnp.concatenate(arrays, axis=along)  13.1 us
  transfers between devices with their start and end apart: 5, of which 2 were waited for; matrix products, arithmetic and copies ran while one was open for 30% of the time, Pallas kernels for 0%

commit v1 on v0

v1 whole, which is shorter than its diff:
```python
import functools
import math

import jax
import jax.numpy as jnp
from jax import lax
from jax.experimental import pallas as pl
from jax.experimental.pallas import tpu as pltpu
from jax.sharding import PartitionSpec as P

MODEL_WIDTH = 4096
HIDDEN_UNITS = 16384
RANK = 4
MEMBERS = 64
S_IN = 0.5 / math.sqrt(MODEL_WIDTH * RANK)
S_OUT = 0.5 / math.sqrt(HIDDEN_UNITS * RANK)
C_STEP = 1.0 / math.sqrt(MEMBERS * RANK)
MESH = pl.DeviceIdType.MESH
F32, BF16 = jnp.float32, jnp.bfloat16
OFF = (0, 1, 2, 3)
ORDER = (
    "P0", "P1", "P2", "P3", "W0", "W1", "Q0", "Q1", "Q2", "Q3",
    "T0", "T1", "B0", "T2", "B1", "T3", "B2", "B3", "C0", "C1",
    "C2", "C3", "U0", "U1", "U2", "U3", "D0", "D1", "D2", "D3",
    "E0", "E1", "E2", "E3", "R0", "R1", "R2", "R3", "F0", "F1",
    "F2", "F3", "K0", "K1", "K2", "K3", "X0", "S0", "S1", "G0",
)
X_FIRST = (True, False, True, False)


def kernel(
    ranks,
    tokens,
    gate_w,
    up_w,
    down_w,
    gate_in,
    up_in,
    down_right,
    gate_out,
    up_out,
    down_left,
    terms,
    left,
    right,
    wgu,
    wd,
    tok,
    infac,
    outfac,
    facz,
    fach,
    facd,
    facx,
    part,
    rs1,
    rsx,
    rsy,
    rs2s,
    rs2r,
    gsum,
    hid,
    tsx,
    trx,
    tacc,
    tsz,
    trz,
    scaled,
    load_sem,
    w_s,
    w_r,
    tok_s,
    tok_r,
    th_s,
    th_r,
    fz_s,
    fz_r,
    fh_s,
    fh_r,
    core_s,
    core_r,
    r1_s,
    r1_r,
    r2_s,
    r2_r,
    hx_s,
    hx_r,
    hy_s,
    hy_r,
    tx_s,
    tx_r,
    tz_s,
    tz_r,
    out_sem,
):
    pop, hdx = lax.axis_index("pop"), lax.axis_index("hid")
    z, xh, c = pop // 4, (pop // 2) % 2, pop % 2
    y, xl = hdx // 2, hdx % 2
    pair, zl = z // 2, z % 2

    def at(z_, xh_, c_, y_, xl_):
        return (z_ * 4 + xh_ * 2 + c_, y_ * 2 + xl_)

    core_peer = at(z, xh, 1 - c, y, xl)
    xl_peer = at(z, xh, c, y, 1 - xl)
    xh_peer = at(z, 1 - xh, c, y, xl)

    def y_peer(d):
        return at(z, xh, c, (y + d) % 4, xl)

    def z_others(k):
        return [1 - zl] if k == 0 else [(zl + v) % 2 for v in range(2)]

    def remote(src, dst, ss, rs, to):
        return pltpu.make_async_remote_copy(
            src_ref=src, dst_ref=dst, send_sem=ss, recv_sem=rs, device_id=to, device_id_type=MESH
        )

    def cols(n, size):
        return pl.ds(pl.multiple_of(n * size, size), size)

    sent = []

    def send(*a):
        d = remote(*a)
        d.start()
        sent.append(d)

    loads = [
        (tokens, tok.at[0, zl, xh]),
        (gate_out, outfac.at[0]),
        (up_out, outfac.at[1]),
        (down_left, outfac.at[2]),
        (gate_w, wgu.at[:, cols(c, 512)]),
        (up_w, wgu.at[:, cols(2 + c, 512)]),
        (gate_in, infac.at[0]),
        (up_in, infac.at[1]),
        (down_w, wd.at[cols(c, 512)]),
        (down_right, infac.at[2]),
    ]
    loads = [pltpu.make_async_copy(s, d, load_sem.at[i]) for i, (s, d) in enumerate(loads)]
    for d in loads:
        d.start()

    barrier = pltpu.get_barrier_semaphore()
    friends = [core_peer, xl_peer, xh_peer] + [y_peer(d) for d in (1, 2, 3)]
    for k in range(4):
        q = (pair + 4 - OFF[k]) % 4
        friends += [at(q * 2 + i, xh, c, y, xl) for i in z_others(k)]
    for f in friends:
        pl.semaphore_signal(barrier, inc=1, device_id=f, device_id_type=MESH)
    pl.semaphore_wait(barrier, len(friends))

    for d in loads[:4]:
        d.wait()

    def to_z(k):
        q = (pair + 4 - OFF[k]) % 4
        return [(v, q * 2 + i, at(q * 2 + i, xh, c, y, xl)) for v, i in enumerate(z_others(k))]

    def own_fac(a):
        return pltpu.make_async_copy(
            outfac.at[a, :, :, cols(z, 2048)], facz.at[a, 0, zl], load_sem.at[10 + a]
        )

    for a in range(3):
        own_fac(a).start()

    def send_fac(a, k, v, z_, to):
        for b in a:
            send(
                outfac.at[b, :, :, cols(z_, 2048)],
                facz.at[b, k, zl],
                fz_s.at[b, k, v],
                fz_r.at[b, k, zl],
                to,
            )

    def stage_p(k):
        for v, z_, to in to_z(k):
            send(tok.at[0, zl, xh], tok.at[k, zl, xh], tok_s.at[k, v], tok_r.at[k, zl], to)

    def stage_q(k):
        for v, z_, to in to_z(k):
            send_fac((0, 1, 2), k, v, z_, to)

    def stage_w(k):
        if k == 0:
            send(gate_w, wgu.at[:, cols(c, 512)], w_s.at[0], w_r.at[0], core_peer)
            send(up_w, wgu.at[:, cols(2 + c, 512)], w_s.at[1], w_r.at[1], core_peer)
        else:
            send(down_w, wd.at[cols(c, 512)], w_s.at[2], w_r.at[2], core_peer)

    token = lax.broadcasted_iota(jnp.int32, (128, 32), 0)
    row = lax.broadcasted_iota(jnp.int32, (128, 32), 1)
    same = (
        (token // 64 == row // 8 % 2)
        & (token // 32 % 2 == (xh + row // 16) % 2)
        & (token // 16 % 2 == row // 4 % 2)
    )

    def nt(a, b):
        return lax.dot_general(a, b, (((1,), (1,)), ((), ())), preferred_element_type=F32)

    def tn(a, b):
        return lax.dot_general(a, b, (((0,), (0,)), ((), ())), preferred_element_type=F32)

    def spread(first):
        lane = lax.broadcasted_iota(jnp.int32, (128, 32), 0)
        rank = lax.broadcasted_iota(jnp.int32, (128, 32), 1) % RANK
        return (lane == rank + first).astype(F32).astype(BF16)

    def in_rows(a, k, core):
        q = (pair + OFF[k]) % 4
        return jnp.concatenate(
            [infac[a, q, :, (xh + i) % 2, core].reshape(16, 512) for i in range(2)], axis=0
        )

    def stage_t(k):
        for i in z_others(k):
            got = tok.at[k, i, xh]
            remote(got, got, tok_s.at[k, 0], tok_r.at[k, i], core_peer).wait_recv()
        both = tok.at[k, :, xh]
        send(both, both, th_s.at[k], th_r.at[k], xh_peer)

    def stage_u(k):
        for a in range(3):
            if k == 0:
                own_fac(a).wait()
            for i in z_others(k):
                got = facz.at[a, k, i]
                remote(got, got, fz_s.at[a, k, 0], fz_r.at[a, k, i], core_peer).wait_recv()
            send(
                facz.at[a, k, :, :, :, cols(1 - xh, 1024)],
                fach.at[a, k],
                fh_s.at[a, k],
                fh_r.at[a, k],
                xh_peer,
            )

    def dense(k):
        for a in range(3):
            remote(fach.at[a, k], fach.at[a, k], fh_s.at[a, k], fh_r.at[a, k], xh_peer).wait_recv()
            own = facz[a, k, :, :, :, cols(xh, 1024)].reshape(16, 1024)
            facd[a, 32 * k : 32 * k + 16, :] = own
            facd[a, 32 * k + 16 : 32 * k + 32, :] = fach[a, k].reshape(16, 1024)

    def my_fac(a, k):
        own = facz[a, k, y // 2, xl, :, cols(xh, 1024)]
        return jnp.where(y % 2 == xh, own, fach[a, k, y // 2, xl])

    def stage_b(k):
        if k == 0:
            for i, at_ in enumerate((cols(1 - c, 512), cols(3 - c, 512))):
                remote(gate_w, wgu.at[:, at_], w_s.at[i], w_r.at[i], core_peer).wait_recv()
        both = tok.at[k, :, 1 - xh]
        remote(both, both, th_s.at[k], th_r.at[k], xh_peer).wait_recv()
        if k == 0:
            for d in loads[4:8]:
                d.wait()
        t = tok[k].reshape(128, 512)
        ext = jnp.zeros((128, 128), F32)
        for a in range(2):
            p = jnp.where(same, nt(t, in_rows(a, k, c)) * S_IN, 0.0).astype(BF16)
            ext += nt(p, spread(4 * a))
            for n in range(2):
                w = slice(1024 * a + 512 * n, 1024 * a + 512 * n + 512)
                v = jnp.dot(t, wgu[:, w], preferred_element_type=F32)
                part[k, :, :, :, w] = v.astype(BF16).reshape(4, 2, 16, 512)
        part[k, :, :, :, 2048:] = ext.astype(BF16).reshape(4, 2, 16, 128)
        if X_FIRST[k]:
            send(part.at[k, :, 1 - xl], rsx.at[k], r2_s.at[k], r2_r.at[k], xl_peer)
            return
        for d in (2, 1, 3):
            send(
                part.at[k, (y + d) % 4],
                rs1.at[k, d - 1],
                r1_s.at[k, d - 1],
                r1_r.at[k, d - 1],
                y_peer(d),
            )

    def stage_c(k):
        if X_FIRST[k]:
            remote(rsx.at[k], rsx.at[k], r2_s.at[k], r2_r.at[k], xl_peer).wait_recv()
            for d in (2, 1, 3):
                o = (y + d) % 4
                rsy[k, d - 1] = (part[k, o, xl].astype(F32) + rsx[k, o].astype(F32)).astype(BF16)
                send(
                    rsy.at[k, d - 1],
                    rs1.at[k, d - 1, 0],
                    r1_s.at[k, d - 1],
                    r1_r.at[k, d - 1],
                    y_peer(d),
                )
            gsum[k] = part[k, y, xl].astype(F32) + rsx[k, y].astype(F32)
            return
        for d in (1, 2, 3):
            remote(
                rs1.at[k, d - 1], rs1.at[k, d - 1], r1_s.at[k, d - 1], r1_r.at[k, d - 1], y_peer(d)
            ).wait_recv()

        def total(m):
            v = part[k, y, m].astype(F32)
            for d in range(3):
                v += rs1[k, d, m].astype(F32)
            return v

        rs2s[k] = total(1 - xl).astype(BF16)
        send(rs2s.at[k], rs2r.at[k], r2_s.at[k], r2_r.at[k], xl_peer)
        gsum[k] = total(xl)

    def stage_d(k):
        v = gsum[k]
        if X_FIRST[k]:
            for d in (1, 2, 3):
                got = rs1.at[k, d - 1, 0]
                remote(got, got, r1_s.at[k, d - 1], r1_r.at[k, d - 1], y_peer(d)).wait_recv()
            for d in range(3):
                v += rs1[k, d, 0].astype(F32)
        else:
            remote(rs2s.at[k], rs2r.at[k], r2_s.at[k], r2_r.at[k], xl_peer).wait_recv()
            v += rs2r[k].astype(F32)
        dense(k)
        g, u = v[:, :1024], v[:, 1024:2048]
        p = v[:, 2048:].astype(BF16)
        g += jnp.dot(p[:, :RANK], my_fac(0, k), preferred_element_type=F32)
        u += jnp.dot(p[:, RANK : 2 * RANK], my_fac(1, k), preferred_element_type=F32)
        h = (g / (1.0 + jnp.exp(-g)) * u).astype(BF16)
        hid[k, y, xl, :, :1024] = h
        p = nt(h, my_fac(2, k)) * S_OUT
        hid[k, y, xl, :, 1024:] = jnp.concatenate(
            [p.astype(BF16), jnp.zeros((16, 124), BF16)], axis=1
        )
        own = hid.at[k, y, xl]
        send(own, own, hx_s.at[k], hx_r.at[k], xl_peer)
        for d in (1, 3):
            send(own, own, hy_s.at[k, 0, d - 1], hy_r.at[k, xl, d - 1], y_peer(d))

    def stage_e(k):
        got = hid.at[k, y, 1 - xl]
        remote(got, got, hx_s.at[k], hx_r.at[k], xl_peer).wait_recv()
        for d in (1, 3):
            send(got, got, hy_s.at[k, 1, d - 1], hy_r.at[k, 1 - xl, d - 1], y_peer(d))

    def from_y(k, m, d):
        got = hid.at[k, (y + 4 - d) % 4, m]
        remote(got, got, hy_s.at[k, 0, 0], hy_r.at[k, m, d - 1], y_peer(d)).wait_recv()
        return got

    def stage_r(k):
        for m, d in ((0, 1), (1, 3)):
            got = from_y(k, m, d)
            send(got, got, hy_s.at[k, m, 1], hy_r.at[k, m, 1], y_peer(d))

    def stage_f(k):
        if k == 0:
            remote(
                down_w, wd.at[cols(1 - c, 512)], w_s.at[2], w_r.at[2], core_peer
            ).wait_recv()
            for d in loads[8:]:
                d.wait()
        for m, d in ((0, 3), (1, 1), (0, 2), (1, 2)):
            from_y(k, m, d)
        h = hid[k].reshape(128, 1152)
        p = jnp.dot(h[:, 1024:], spread(0), preferred_element_type=F32)
        p = jnp.where(same, p, 0.0).astype(BF16)
        v = jnp.dot(h[:, :1024], wd[...], preferred_element_type=F32)
        v += jnp.dot(p, in_rows(2, k, c), preferred_element_type=F32)
        v = v.reshape(2, 2, 32, 512)

        def rows(away):
            return jnp.where(xh == away, v[:, 1], v[:, 0])

        tsx[k] = rows(0).astype(BF16)
        tacc[k] = rows(1)
        send(tsx.at[k], trx.at[k], tx_s.at[k], tx_r.at[k], xh_peer)

    def stage_k(k):
        remote(tsx.at[k], trx.at[k], tx_s.at[k], tx_r.at[k], xh_peer).wait_recv()
        tsz[k] = (tacc[k] + trx[k].astype(F32)).astype(BF16)
        q = (pair + OFF[k]) % 4
        for v, i in enumerate(z_others(k)):
            to = at(q * 2 + i, xh, c, y, xl)
            send(tsz.at[k, i], trz.at[k, zl], tz_s.at[k, v], tz_r.at[k, zl], to)

    def stage_x():
        for a in range(3):
            send(
                facd.at[a, :, cols(1 - c, 512)],
                facx.at[a],
                core_s.at[a],
                core_r.at[a],
                core_peer,
            )

    def outs(a):
        return [
            pltpu.make_async_copy(facd.at[a, :, cols(c, 512)], left.at[a, 0], out_sem.at[a, 0]),
            pltpu.make_async_copy(facx.at[a], left.at[a, 1], out_sem.at[a, 1]),
            pltpu.make_async_copy(scaled.at[a], right.at[a], out_sem.at[a, 2]),
        ]

    def stage_s(part_):
        member = lax.broadcasted_iota(jnp.int32, (32, 1), 0) // 4
        if part_ == 1:
            for a in range(3):
                remote(
                    facx.at[a], facx.at[a], core_s.at[a], core_r.at[a], core_peer
                ).wait_recv()
                for d in outs(a):
                    d.start()
            return
        for k in range(4):
            for i in range(2):
                core = (c + i) % 2
                q = (pair + OFF[k]) % 4
                r = jnp.zeros((32, 1), F32)
                for m in range(8):
                    who = q * 16 + (m // 2 % 2) * 8 + core * 2 + m % 2
                    who += 4 * ((xh + m // 4) % 2)
                    r = jnp.where(member == m, ranks[who].astype(F32), r)
                fit = r / (MEMBERS - 1.0) - 0.5
                for a in range(3):
                    scaled[a, i, 32 * k : 32 * k + 32, :] = (
                        in_rows(a, k, core).astype(F32) * fit
                    ).astype(BF16)

    def stage_g():
        own = pltpu.make_async_copy(tsz.at[0, zl], trz.at[0, zl], load_sem.at[13])
        own.start()
        for k in range(4):
            for i in z_others(k):
                got = trz.at[k, i]
                remote(got, got, tz_s.at[k, 0], tz_r.at[k, i], core_peer).wait_recv()
        own.wait()
        done = pltpu.make_async_copy(trz, terms, load_sem.at[14])
        done.start()
        for a in range(3):
            for d in outs(a):
                d.wait()
        done.wait()

    stages = dict(P=stage_p, Q=stage_q, W=stage_w, T=stage_t, U=stage_u, B=stage_b)
    stages.update(C=stage_c, D=stage_d, E=stage_e, R=stage_r, F=stage_f, K=stage_k, S=stage_s)
    final = dict(X=stage_x, G=stage_g)
    for name in ORDER:
        if name[0] in stages:
            stages[name[0]](int(name[1]))
        else:
            final[name[0]]()
    for d in sent:
        d.wait_send()


def finish(terms, left, right, mixed, gate_step, up_step, down_step, tv, lv, rv, steps, in_sem, sem):
    loads = [
        (pltpu.make_async_copy(left.at[a], lv.at[a], in_sem.at[a, 0]),
         pltpu.make_async_copy(right.at[a], rv.at[a], in_sem.at[a, 1]))
        for a in range(3)
    ]
    last = pltpu.make_async_copy(terms, tv, in_sem.at[3, 0])
    for l, r in loads:
        l.start()
        r.start()
    last.start()
    copies = []
    for a, out in enumerate((gate_step, up_step, down_step)):
        for d in loads[a]:
            d.wait()
        x, y = (rv, lv) if a < 2 else (lv, rv)
        steps[a] = C_STEP * lax.dot_general(
            x[a], y[a], (((0,), (0,)), ((), ())), preferred_element_type=F32
        )
        copies.append(pltpu.make_async_copy(steps.at[a], out, sem.at[a]))
        copies[a].start()
    last.wait()
    v = tv[0].astype(F32)
    for i in range(1, 8):
        v += tv[i].astype(F32)
    mixed[...] = v.astype(BF16)
    for d in copies:
        d.wait()


def local(
    tokens,
    fitness_ranks,
    gate_weight,
    up_weight,
    down_weight,
    gate_input_factor,
    up_input_factor,
    down_right,
    gate_output_factor,
    up_output_factor,
    down_left,
):
    def grouped(x):
        return x.reshape(4, 2, 2, 2, 2, RANK, 512)

    dma = pltpu.SemaphoreType.DMA
    big = jax.ShapeDtypeStruct((512, 512), F32)
    any_ = pl.BlockSpec(memory_space=pl.ANY)
    terms, left, right = (
        pl.pallas_call(
            kernel,
            out_shape=(
                jax.ShapeDtypeStruct((4, 2, 32, 512), BF16),
                jax.ShapeDtypeStruct((3, 2, 128, 512), BF16),
                jax.ShapeDtypeStruct((3, 2, 128, 512), BF16),
            ),
            in_specs=[pl.BlockSpec(memory_space=pltpu.SMEM)] + [any_] * 10,
            out_specs=(any_, any_, any_),
            scratch_shapes=[
                pltpu.VMEM((512, 2048), BF16),
                pltpu.VMEM((1024, 512), BF16),
                pltpu.VMEM((4, 2, 2, 32, 512), BF16),
                pltpu.VMEM((3, 4, 2, 2, 2, 2, RANK, 512), BF16),
                pltpu.VMEM((3, 2, RANK, HIDDEN_UNITS), BF16),
                pltpu.VMEM((3, 4, 2, 2, RANK, 2048), BF16),
                pltpu.VMEM((3, 4, 2, 2, RANK, 1024), BF16),
                pltpu.VMEM((3, 128, 1024), BF16),
                pltpu.VMEM((3, 128, 512), BF16),
                pltpu.VMEM((4, 4, 2, 16, 2176), BF16),
                pltpu.VMEM((4, 3, 2, 16, 2176), BF16),
                pltpu.VMEM((4, 4, 16, 2176), BF16),
                pltpu.VMEM((4, 3, 16, 2176), BF16),
                pltpu.VMEM((4, 16, 2176), BF16),
                pltpu.VMEM((4, 16, 2176), BF16),
                pltpu.VMEM((4, 16, 2176), F32),
                pltpu.VMEM((4, 4, 2, 16, 1152), BF16),
                pltpu.VMEM((4, 2, 32, 512), BF16),
                pltpu.VMEM((4, 2, 32, 512), BF16),
                pltpu.VMEM((4, 2, 32, 512), F32),
                pltpu.VMEM((4, 2, 32, 512), BF16),
                pltpu.VMEM((4, 2, 32, 512), BF16),
                pltpu.VMEM((3, 2, 128, 512), BF16),
                dma((15,)),
                dma((3,)),
                dma((3,)),
                dma((4, 2)),
                dma((4, 2)),
                dma((4,)),
                dma((4,)),
                dma((3, 4, 2)),
                dma((3, 4, 2)),
                dma((3, 4)),
                dma((3, 4)),
                dma((3,)),
                dma((3,)),
                dma((4, 3)),
                dma((4, 3)),
                dma((4,)),
                dma((4,)),
                dma((4,)),
                dma((4,)),
                dma((4, 2, 3)),
                dma((4, 2, 3)),
                dma((4,)),
                dma((4,)),
                dma((4, 2)),
                dma((4, 2)),
                dma((3, 3)),
            ],
            compiler_params=pltpu.CompilerParams(
                collective_id=0, has_side_effects=True, vmem_limit_bytes=56 * 2**20
            ),
        )(
            fitness_ranks,
            tokens,
            gate_weight,
            up_weight,
            down_weight,
            grouped(gate_input_factor),
            grouped(up_input_factor),
            grouped(down_right),
            gate_output_factor,
            up_output_factor,
            down_left,
        )
    )
    vmem = pl.BlockSpec(memory_space=pltpu.VMEM)
    return pl.pallas_call(
        finish,
        out_shape=(jax.ShapeDtypeStruct((32, 512), BF16), big, big, big),
        in_specs=[any_] * 3,
        out_specs=(vmem, any_, any_, any_),
        scratch_shapes=[
            pltpu.VMEM((8, 32, 512), BF16),
            pltpu.VMEM((3, 256, 512), BF16),
            pltpu.VMEM((3, 256, 512), BF16),
            pltpu.VMEM((3, 512, 512), F32),
            dma((4, 2)),
            dma((3,)),
        ],
        compiler_params=pltpu.CompilerParams(vmem_limit_bytes=60 * 2**20),
    )(terms.reshape(8, 32, 512), left.reshape(3, 256, 512), right.reshape(3, 256, 512))


def solution(mesh):
    in_specs = (
        P("pop", "hid"),
        P(),
        P("hid", "pop"),
        P("hid", "pop"),
        P("pop", "hid"),
        P(None, None, "hid"),
        P(None, None, "hid"),
        P(None, None, "hid"),
        P("pop", None, None),
        P("pop", None, None),
        P("pop", None, None),
    )
    out_specs = (P("pop", "hid"), P("hid", "pop"), P("hid", "pop"), P("pop", "hid"))
    return jax.shard_map(local, mesh=mesh, in_specs=in_specs, out_specs=out_specs, check_vma=False)
```

time: 266 us -> 74.7 us (0.28)
  local copies, waits for them, and re-layouts: 77.6 us -> 0 us
  Pallas kernels: 0 us -> 74 us
  blocking collectives: 69.5 us -> 0 us
  waiting for transfers between devices: 51.7 us -> 0 us
  starting transfers between devices: 33.9 us -> 0 us
  matrix products: 14 us -> 0 us
  between operations: 14.3 us -> 0.64 us
  other arithmetic: 2.82 us -> 0 us
    pallas_call x0 -> x2, Pallas kernels: none -> 74 us  [the longest x1 70.2 us: local(): pl.pallas_call(kernel, out_shape=(jax.ShapeDtypeStruct((4, 2, 32, 512), B...]
    all_to_all x4 -> x0, waiting for transfers between devices: 51.7 us -> none  [the longest x2 28 us: copy_for_each(): return lax.all_to_all(copies, axis, split_axis=0, concat_axis=0, tiled=True)]
    all_gather x1 -> x0, blocking collectives: 48.4 us -> none  [in_one_piece(): lax.all_gather(both, axis, axis=dim, tiled=True)]
    unnamed x27 -> x0, local copies, waits for them, and re-layouts: 42.1 us -> none
    all_to_all x4 -> x0, starting transfers between devices: 33.9 us -> none  [the longest x2 15.7 us: copy_for_each(): return lax.all_to_all(copies, axis, split_axis=0, concat_axis=0, tiled=True)]
    all_to_all x1 -> x0, blocking collectives: 21.1 us -> none  [copy_for_each(): return lax.all_to_all(copies, axis, split_axis=0, concat_axis=0, tiled=True)]
    all_to_all x1 -> x0, local copies, waits for them, and re-layouts: 17.9 us -> none  [sent_together(): lax.all_to_all(both, axis, split_axis=split_dim, concat_axis=concat_dim,...]
    dot_general x10 -> x0, matrix products: 14 us -> none  [the longest x1 3.27 us: local(): jnp.dot(picked, down_weight, preferred_element_type=scalar_real)]
  transfers between devices with their start and end apart: 5 -> 0, of which waited for: 2 -> 0; matrix products, arithmetic and copies ran while one was open for 30% -> 0% of each run, Pallas kernels for 0% -> 0%
where the time goes in v1:
time: 74.7 us; the launch traced here: 74.6 us
  Pallas kernels  74 us (99%)
    pallas_call x1, Pallas kernels, local(): pl.pallas_call(kernel, out_shape=(jax.ShapeDtypeStruct((4, 2, 32, 512), B...  70.2 us
    pallas_call x1, Pallas kernels, local(): pl.pallas_call(finish, out_shape=(jax.ShapeDtypeStruct((32, 512), BF16),...  3.73 us

profile of v1, /device:TPU:32, one launch (start us, length us, event | category | flops | bytes accessed | tf_op | source)
XLA Modules:
  0.0 74.6 jit_solution(404539815638750592)
XLA Ops:
  0.6 70.2 %shard_map.138 = (bf16[4,2,32,512]{3,2,1,0:T(8,128)(2,1)}, bf16[3,2,128,512]{3,2,1,0:T(8,128)(2,1)}, bf16[3,2,128,512]{3,2,1,0:T(8,128)(2,1)}) custom-call(s32[64]{0:T(128)} %ranks.1, bf16[32,512]{1,0:T(8,128)(2,1)} %tokens.1, bf16[512,512]{1,0:T(8,128)(2,1)} %gate_w.1, bf16[512,512]{1,0:T(8,128)(2,1)} %up_w.1, bf16[512,512]{1,0:T(8,128)(2,1)} %down_w.1, ...), custom_call_target="tpu_custom_call" | custom-call | tf_op jit(solution)/shard_map/pallas_call | solution.py:506
  70.9 3.7 %shard_map.139 = (bf16[32,512]{1,0:T(8,128)(2,1)}, f32[512,512]{1,0:T(8,128)}, f32[512,512]{1,0:T(8,128)}, f32[512,512]{1,0:T(8,128)}) custom-call(bf16[8,32,512]{2,1,0:T(8,128)(2,1)} %bitcast.8, bf16[3,256,512]{2,1,0:T(8,128)(2,1)} %bitcast.6, bf16[3,256,512]{2,1,0:T(8,128)(2,1)} %bitcast.7), custom_call_target="tpu_custom_call" | custom-call | tf_op jit(solution)/shard_map/pallas_call | solution.py:584

commit v2 on v1

--- a/solution.py
+++ b/solution.py
@@ -20,10 +20,10 @@
 OFF = (0, 1, 2, 3)
 ORDER = (
     "P0", "P1", "P2", "P3", "W0", "W1", "Q0", "Q1", "Q2", "Q3",
-    "T0", "T1", "B0", "T2", "B1", "T3", "B2", "B3", "C0", "C1",
-    "C2", "C3", "U0", "U1", "U2", "U3", "D0", "D1", "D2", "D3",
-    "E0", "E1", "E2", "E3", "R0", "R1", "R2", "R3", "F0", "F1",
-    "F2", "F3", "K0", "K1", "K2", "K3", "X0", "S0", "S1", "G0",
+    "T0", "T1", "B0", "T2", "B1", "T3", "B2", "B3", "U0", "C0",
+    "U1", "C1", "U2", "C2", "U3", "C3", "D0", "D1", "D2", "D3",
+    "X0", "S0", "E0", "E1", "E2", "E3", "R0", "R1", "R2", "R3",
+    "F0", "F1", "F2", "F3", "S1", "K0", "K1", "K2", "K3", "G0",
 )
 X_FIRST = (True, False, True, False)
 
@@ -41,8 +41,7 @@
     up_out,
     down_left,
     terms,
-    left,
-    right,
+    made,
     wgu,
     wd,
     tok,
@@ -66,6 +65,7 @@
     tsz,
     trz,
     scaled,
+    steps,
     load_sem,
     w_s,
     w_r,
@@ -238,12 +238,9 @@
                 xh_peer,
             )
 
-    def dense(k):
+    def other_half(k):
         for a in range(3):
             remote(fach.at[a, k], fach.at[a, k], fh_s.at[a, k], fh_r.at[a, k], xh_peer).wait_recv()
-            own = facz[a, k, :, :, :, cols(xh, 1024)].reshape(16, 1024)
-            facd[a, 32 * k : 32 * k + 16, :] = own
-            facd[a, 32 * k + 16 : 32 * k + 32, :] = fach[a, k].reshape(16, 1024)
 
     def my_fac(a, k):
         own = facz[a, k, y // 2, xl, :, cols(xh, 1024)]
@@ -256,7 +253,7 @@
         both = tok.at[k, :, 1 - xh]
         remote(both, both, th_s.at[k], th_r.at[k], xh_peer).wait_recv()
         if k == 0:
-            for d in loads[4:8]:
+            for d in loads[4:]:
                 d.wait()
         t = tok[k].reshape(128, 512)
         ext = jnp.zeros((128, 128), F32)
@@ -321,7 +318,7 @@
         else:
             remote(rs2s.at[k], rs2r.at[k], r2_s.at[k], r2_r.at[k], xl_peer).wait_recv()
             v += rs2r[k].astype(F32)
-        dense(k)
+        other_half(k)
         g, u = v[:, :1024], v[:, 1024:2048]
         p = v[:, 2048:].astype(BF16)
         g += jnp.dot(p[:, :RANK], my_fac(0, k), preferred_element_type=F32)
@@ -358,8 +355,6 @@
             remote(
                 down_w, wd.at[cols(1 - c, 512)], w_s.at[2], w_r.at[2], core_peer
             ).wait_recv()
-            for d in loads[8:]:
-                d.wait()
         for m, d in ((0, 3), (1, 1), (0, 2), (1, 2)):
             from_y(k, m, d)
         h = hid[k].reshape(128, 1152)
@@ -386,6 +381,10 @@
 
     def stage_x():
         for a in range(3):
+            for k in range(4):
+                own = facz[a, k, :, :, :, cols(xh, 1024)].reshape(16, 1024)
+                facd[a, 32 * k : 32 * k + 16, :] = own
+                facd[a, 32 * k + 16 : 32 * k + 32, :] = fach[a, k].reshape(16, 1024)
             send(
                 facd.at[a, :, cols(1 - c, 512)],
                 facx.at[a],
@@ -395,11 +394,7 @@
             )
 
     def outs(a):
-        return [
-            pltpu.make_async_copy(facd.at[a, :, cols(c, 512)], left.at[a, 0], out_sem.at[a, 0]),
-            pltpu.make_async_copy(facx.at[a], left.at[a, 1], out_sem.at[a, 1]),
-            pltpu.make_async_copy(scaled.at[a], right.at[a], out_sem.at[a, 2]),
-        ]
+        return pltpu.make_async_copy(steps.at[a], made.at[a], out_sem.at[a])
 
     def stage_s(part_):
         member = lax.broadcasted_iota(jnp.int32, (32, 1), 0) // 4
@@ -408,8 +403,14 @@
                 remote(
                     facx.at[a], facx.at[a], core_s.at[a], core_r.at[a], core_peer
                 ).wait_recv()
-                for d in outs(a):
-                    d.start()
+                v = None
+                for i in range(2):
+                    f = facd[a, :, cols(c, 512)] if i == 0 else facx[a]
+                    x = scaled[a, i]
+                    w = tn(x, f) if a < 2 else tn(f, x)
+                    v = w if v is None else v + w
+                steps[a] = v * C_STEP
+                outs(a).start()
             return
         for k in range(4):
             for i in range(2):
@@ -437,8 +438,7 @@
         done = pltpu.make_async_copy(trz, terms, load_sem.at[14])
         done.start()
         for a in range(3):
-            for d in outs(a):
-                d.wait()
+            outs(a).wait()
         done.wait()
 
     stages = dict(P=stage_p, Q=stage_q, W=stage_w, T=stage_t, U=stage_u, B=stage_b)
@@ -453,33 +453,30 @@
         d.wait_send()
 
 
-def finish(terms, left, right, mixed, gate_step, up_step, down_step, tv, lv, rv, steps, in_sem, sem):
+def finish(terms, made, mixed, gate_step, up_step, down_step, tv, held, in_sem, sem, out_sem):
+    load = pltpu.make_async_copy(terms, tv, in_sem)
+    load.start()
+    pieces = [(a, i, pl.ds(128 * i, 128)) for a in range(3) for i in range(4)]
     loads = [
-        (pltpu.make_async_copy(left.at[a], lv.at[a], in_sem.at[a, 0]),
-         pltpu.make_async_copy(right.at[a], rv.at[a], in_sem.at[a, 1]))
-        for a in range(3)
+        pltpu.make_async_copy(made.at[a, rows], held.at[a, rows], sem.at[a, i])
+        for a, i, rows in pieces
     ]
-    last = pltpu.make_async_copy(terms, tv, in_sem.at[3, 0])
-    for l, r in loads:
-        l.start()
-        r.start()
-    last.start()
-    copies = []
-    for a, out in enumerate((gate_step, up_step, down_step)):
-        for d in loads[a]:
-            d.wait()
-        x, y = (rv, lv) if a < 2 else (lv, rv)
-        steps[a] = C_STEP * lax.dot_general(
-            x[a], y[a], (((0,), (0,)), ((), ())), preferred_element_type=F32
-        )
-        copies.append(pltpu.make_async_copy(steps.at[a], out, sem.at[a]))
-        copies[a].start()
-    last.wait()
+    for d in loads:
+        d.start()
+    outs = (gate_step, up_step, down_step)
+    stores = [
+        pltpu.make_async_copy(held.at[a, rows], outs[a].at[rows], out_sem.at[a, i])
+        for a, i, rows in pieces
+    ]
+    for l, d in zip(loads, stores):
+        l.wait()
+        d.start()
+    load.wait()
     v = tv[0].astype(F32)
     for i in range(1, 8):
         v += tv[i].astype(F32)
     mixed[...] = v.astype(BF16)
-    for d in copies:
+    for d in stores:
         d.wait()
 
 
@@ -502,16 +499,15 @@
     dma = pltpu.SemaphoreType.DMA
     big = jax.ShapeDtypeStruct((512, 512), F32)
     any_ = pl.BlockSpec(memory_space=pl.ANY)
-    terms, left, right = (
+    terms, made = (
         pl.pallas_call(
             kernel,
             out_shape=(
                 jax.ShapeDtypeStruct((4, 2, 32, 512), BF16),
-                jax.ShapeDtypeStruct((3, 2, 128, 512), BF16),
-                jax.ShapeDtypeStruct((3, 2, 128, 512), BF16),
+                jax.ShapeDtypeStruct((3, 512, 512), F32),
             ),
             in_specs=[pl.BlockSpec(memory_space=pltpu.SMEM)] + [any_] * 10,
-            out_specs=(any_, any_, any_),
+            out_specs=(any_, any_),
             scratch_shapes=[
                 pltpu.VMEM((512, 2048), BF16),
                 pltpu.VMEM((1024, 512), BF16),
@@ -536,6 +532,7 @@
                 pltpu.VMEM((4, 2, 32, 512), BF16),
                 pltpu.VMEM((4, 2, 32, 512), BF16),
                 pltpu.VMEM((3, 2, 128, 512), BF16),
+                pltpu.VMEM((3, 512, 512), F32),
                 dma((15,)),
                 dma((3,)),
                 dma((3,)),
@@ -561,7 +558,7 @@
                 dma((4,)),
                 dma((4, 2)),
                 dma((4, 2)),
-                dma((3, 3)),
+                dma((3,)),
             ],
             compiler_params=pltpu.CompilerParams(
                 collective_id=0, has_side_effects=True, vmem_limit_bytes=56 * 2**20
@@ -584,18 +581,17 @@
     return pl.pallas_call(
         finish,
         out_shape=(jax.ShapeDtypeStruct((32, 512), BF16), big, big, big),
-        in_specs=[any_] * 3,
+        in_specs=[any_] * 2,
         out_specs=(vmem, any_, any_, any_),
         scratch_shapes=[
             pltpu.VMEM((8, 32, 512), BF16),
-            pltpu.VMEM((3, 256, 512), BF16),
-            pltpu.VMEM((3, 256, 512), BF16),
             pltpu.VMEM((3, 512, 512), F32),
-            dma((4, 2)),
-            dma((3,)),
+            dma(()),
+            dma((3, 4)),
+            dma((3, 4)),
         ],
         compiler_params=pltpu.CompilerParams(vmem_limit_bytes=60 * 2**20),
-    )(terms.reshape(8, 32, 512), left.reshape(3, 256, 512), right.reshape(3, 256, 512))
+    )(terms.reshape(8, 32, 512), made)
 
 
 def solution(mesh):

time: 74.7 us -> 72.5 us (0.971)
  Pallas kernels: 74 us -> 71.6 us
    pallas_call x1, Pallas kernels: 70.2 us -> 68.1 us  [local(): pl.pallas_call(kernel, out_shape=(jax.ShapeDtypeStruct((4, 2, 32, 512), B...]
where the time goes in v2:
time: 72.5 us; the launch traced here: 72.3 us
  Pallas kernels  71.6 us (99%)
    pallas_call x1, Pallas kernels, local(): pl.pallas_call(kernel, out_shape=(jax.ShapeDtypeStruct((4, 2, 32, 512), B...  68.1 us
    pallas_call x1, Pallas kernels, local(): pl.pallas_call(finish, out_shape=(jax.ShapeDtypeStruct((32, 512), BF16),...  3.58 us

profile of v2, /device:TPU:32, one launch (start us, length us, event | category | flops | bytes accessed | tf_op | source)
XLA Modules:
  0.0 72.3 jit_solution(11677313742767091624)
XLA Ops:
  0.6 68.1 %shard_map.138 = (bf16[4,2,32,512]{3,2,1,0:T(8,128)(2,1)}, f32[3,512,512]{2,1,0:T(8,128)}) custom-call(s32[64]{0:T(128)} %ranks.1, bf16[32,512]{1,0:T(8,128)(2,1)} %tokens.1, bf16[512,512]{1,0:T(8,128)(2,1)} %gate_w.1, bf16[512,512]{1,0:T(8,128)(2,1)} %up_w.1, bf16[512,512]{1,0:T(8,128)(2,1)} %down_w.1, bf16[4,2,2,2,2,4,512]{6,5,4,3,2,1,0:T(4,128)(2,1)} %bitcast.4, ...), custom_call_target="tpu_custom_call" | custom-call | tf_op jit(solution)/shard_map/pallas_call | solution.py:503
  68.7 3.6 %shard_map.139 = (bf16[32,512]{1,0:T(8,128)(2,1)}, f32[512,512]{1,0:T(8,128)}, f32[512,512]{1,0:T(8,128)}, f32[512,512]{1,0:T(8,128)}) custom-call(bf16[8,32,512]{2,1,0:T(8,128)(2,1)} %bitcast.7, f32[3,512,512]{2,1,0:T(8,128)} %get-tuple-element.7.made), custom_call_target="tpu_custom_call" | custom-call | tf_op jit(solution)/shard_map/pallas_call | solution.py:581

commit v3 on v2

--- a/solution.py
+++ b/solution.py
@@ -25,7 +25,7 @@
     "X0", "S0", "E0", "E1", "E2", "E3", "R0", "R1", "R2", "R3",
     "F0", "F1", "F2", "F3", "S1", "K0", "K1", "K2", "K3", "G0",
 )
-X_FIRST = (True, False, True, False)
+X_FIRST = (False, False, True, False)
 
 
 def kernel(

time: 72.5 us -> 70.8 us (0.977)
  Pallas kernels: 71.6 us -> 70 us
    pallas_call x1, Pallas kernels: 68.1 us -> 66.4 us  [local(): pl.pallas_call(kernel, out_shape=(jax.ShapeDtypeStruct((4, 2, 32, 512), B...]
where the time goes in v3:
time: 70.8 us; the launch traced here: 70.7 us
  Pallas kernels  70 us (99%)
    pallas_call x1, Pallas kernels, local(): pl.pallas_call(kernel, out_shape=(jax.ShapeDtypeStruct((4, 2, 32, 512), B...  66.4 us
    pallas_call x1, Pallas kernels, local(): pl.pallas_call(finish, out_shape=(jax.ShapeDtypeStruct((32, 512), BF16),...  3.58 us

profile of v3, /device:TPU:32, one launch (start us, length us, event | category | flops | bytes accessed | tf_op | source)
XLA Modules:
  0.0 70.7 jit_solution(12631087234208658516)
XLA Ops:
  0.6 66.4 %shard_map.138 = (bf16[4,2,32,512]{3,2,1,0:T(8,128)(2,1)}, f32[3,512,512]{2,1,0:T(8,128)}) custom-call(s32[64]{0:T(128)} %ranks.1, bf16[32,512]{1,0:T(8,128)(2,1)} %tokens.1, bf16[512,512]{1,0:T(8,128)(2,1)} %gate_w.1, bf16[512,512]{1,0:T(8,128)(2,1)} %up_w.1, bf16[512,512]{1,0:T(8,128)(2,1)} %down_w.1, bf16[4,2,2,2,2,4,512]{6,5,4,3,2,1,0:T(4,128)(2,1)} %bitcast.4, ...), custom_call_target="tpu_custom_call" | custom-call | tf_op jit(solution)/shard_map/pallas_call | solution.py:503
  67.1 3.6 %shard_map.139 = (bf16[32,512]{1,0:T(8,128)(2,1)}, f32[512,512]{1,0:T(8,128)}, f32[512,512]{1,0:T(8,128)}, f32[512,512]{1,0:T(8,128)}) custom-call(bf16[8,32,512]{2,1,0:T(8,128)(2,1)} %bitcast.7, f32[3,512,512]{2,1,0:T(8,128)} %get-tuple-element.7.made), custom_call_target="tpu_custom_call" | custom-call | tf_op jit(solution)/shard_map/pallas_call | solution.py:581
